TPU v7x, 128 devices: a whole 4x4x4 slice. The times are simulated.
128 devices in a mesh: ctx: 16 (over z, x_hi, core), samp: 4 (over y), tp: 2 (over x_lo).
Axes of the slice: x: 4 (x_hi: 2, x_lo: 2; x = x_hi * 2 + x_lo), y: 4, z: 4, core: 2. Of those that a mesh axis runs over, the one named last changes fastest.
Arguments:
- queries: bfloat16 [64, 256, 6144], P(('ctx', 'samp'), None, 'tp'), may hold values from -4.5 to 4.5
- out_grad: bfloat16 [64, 256, 6144], P(('ctx', 'samp'), None, 'tp'), may hold values from -12 to 12
- answer_kv: bfloat16 [64, 256, 256], P(('ctx', 'samp')), may hold values from -4.5 to 4.5
- prompt_kv: bfloat16 [4, 1024, 256], P(None, 'ctx'), may hold values from -4.5 to 4.5
- answer_prompt: int32 [64], P(('ctx', 'samp')), may hold values from 0 to 3, as said below
- answer_len: int32 [64], P(('ctx', 'samp')), may hold values from 32 to 256
Outputs:
- query_grad: float32 [64, 256, 6144], P(('ctx', 'samp'), None, 'tp')
- answer_kv_grad: float32 [64, 256, 256], P(('ctx', 'samp'))
- prompt_kv_grad: float32 [4, 1024, 256], P(None, 'ctx')
Inputs may be any that keep to these rules, and one draw needn't show every extreme that they name: `answer_prompt`: every one of the 4 prompts is continued by at least one answer.
All inputs are finite; a program needn't handle non-finite values.
Results may differ from a plain program's by a relative error of at most 0.02.
Values may be sent and summed in bfloat16 or wider, within the bound.
A program may use at most 192 MiB of HBM per device.

v0:
```python
import functools

import jax
import jax.numpy as jnp
from jax import lax
from jax.experimental import pallas as pl
from jax.experimental.pallas import tpu as pltpu
from jax.sharding import PartitionSpec as P

BF = jnp.bfloat16
F32 = jnp.float32
T = 256
D = 128
PK = 1024
NK = PK + T
NP = 4
NC = 16
BL = PK // NC
NG = 8
SCALE = D**-0.5
EXP2 = SCALE * 1.4426950408889634
RC = 32
MESH = pl.DeviceIdType.MESH
VM = pl.BlockSpec(memory_space=pltpu.VMEM)
SM = pl.BlockSpec(memory_space=pltpu.SMEM)


def one_hot_tile(prompt):
    rows = lax.broadcasted_iota(jnp.int32, (8, 128), 0)
    return jnp.where(rows == prompt, 1.0, 0.0).astype(F32)


def weight_row(tile, prompt):
    row = tile[prompt : prompt + 1, :]
    return jnp.concatenate([row, row], axis=1)


def head_cols(h):
    return pl.ds(pl.multiple_of(h * D, D), D)


def head_rows(h):
    return pl.ds(pl.multiple_of(h * T, T), T)


def prepare(h, q_ref, g_ref, qt, gt, live):
    rows = lax.broadcasted_iota(jnp.int32, (T, D), 0)
    g = jnp.where(rows < live, g_ref[:, head_cols(h)].astype(F32), 0.0).astype(BF)
    g_ref[:, head_cols(h)] = g
    qt[:, head_rows(h)] = q_ref[:, head_cols(h)].T
    gt[:, head_rows(h)] = g.T


def scaled_halves(keys):
    scaled = keys.astype(F32) * EXP2
    high = scaled.astype(BF)
    low = (scaled - high.astype(F32)).astype(BF)
    return jnp.concatenate([high, low], axis=1)


def twice(q):
    return jnp.concatenate([q, q], axis=1)


def own_products(h, q_ref, g_ref, kt, vt, s_own, d_own, probs, dscores):
    s = jnp.dot(twice(q_ref[:, head_cols(h)]), kt[:, PK:], preferred_element_type=F32)
    row = lax.broadcasted_iota(jnp.int32, (T, T), 0)
    col = lax.broadcasted_iota(jnp.int32, (T, T), 1)
    s_own[h] = jnp.where(row >= col, s, -jnp.inf)
    d_own[h] = jnp.dot(g_ref[:, head_cols(h)], vt[:, PK:], preferred_element_type=F32)
    top_rows = pl.ds(pl.multiple_of(h * T, T), T // 2)
    probs[top_rows, PK + T // 2 :] = jnp.zeros((T // 2, T // 2), BF)
    dscores[top_rows, PK + T // 2 :] = jnp.zeros((T // 2, T // 2), BF)


def products(h, q_ref, g_ref, kt, vt, s_buf, d_buf):
    s_buf[...] = jnp.dot(twice(q_ref[:, head_cols(h)]), kt[:, :PK], preferred_element_type=F32)
    d_buf[...] = jnp.dot(g_ref[:, head_cols(h)], vt[:, :PK], preferred_element_type=F32)


def softmax_terms(h, s_buf, d_buf, s_own, d_own, probs, dscores):
    for r in range(T // RC):
        r0 = r * RC
        own = 128 if r0 < 128 else 256
        rows = slice(r0, r0 + RC)
        out_rows = pl.ds(pl.multiple_of(h * T + r0, RC), RC)
        s = jnp.concatenate([s_buf[rows, :], s_own[h, rows, :own]], axis=1)
        top = jnp.max(s, axis=1, keepdims=True)
        e = jnp.exp2(s - top)
        p = e * (1.0 / jnp.sum(e, axis=1, keepdims=True))
        probs[out_rows, : PK + own] = p.astype(BF)
        d = jnp.concatenate([d_buf[rows, :], d_own[h, rows, :own]], axis=1)
        delta = jnp.sum(p * d, axis=1, keepdims=True)
        dscores[out_rows, : PK + own] = (p * (d - delta)).astype(BF)


CTX_STEPS = [(dz, dx, dc) for dz in (2, 1, 3, 0) for dx in (1, 0) for dc in (1, 0)]
OWN = len(CTX_STEPS) - 1
SAMP_STEPS = (2, 1, 3, 0)
MEMBERS = [(dy, dt) for dy in (2, 1, 3, 0) for dt in (1, 0)][:-1]
UNROLL = 6
GROUP = 4
PIECE = BL // 4


def fused_kernel(
    heads, len_ref, ap_ref, q_hbm, g_hbm, akv_hbm, pkv_hbm,
    dq, prompt_out, answer_out,
    akv_ref, pkv_ref, q_ref, g_ref, qt, gt, kt, vt, keys, d1, s_own, d_own, probs, dscores,
    hot, hot_all, pick, chosen, grads, land, part, parts, mine_kv, mate_kv,
    load_sem, hs, hr, ps, pr, ts, tr, bs, br, ms, mr, xs, xr,
):
    s0, s1, d0 = (dq.at[:, pl.ds(i * PK, PK)] for i in range(3))
    ctx = lax.axis_index("ctx")
    samp = lax.axis_index("samp")
    tp = lax.axis_index("tp")
    z = ctx // 4
    xh = lax.rem(ctx // 2, 2)
    core = lax.rem(ctx, 2)

    def ctx_at(dz, dx, dc):
        return lax.rem(z + dz, 4) * 4 + lax.rem(xh + dx, 2) * 2 + lax.rem(core + dc, 2)

    def tp_at(dx):
        return lax.rem(tp + dx, 2)

    def samp_at(dy):
        return lax.rem(samp + dy, 4)

    def at(dz, dx, dc, dy=0):
        return {"ctx": ctx_at(dz, dx, dc), "samp": samp_at(dy), "tp": tp_at(dx)}

    def member(dy, dt):
        return {"samp": samp_at(dy), "tp": tp_at(dt)}

    barrier = pltpu.get_barrier_semaphore()
    for step in CTX_STEPS[:OWN]:
        pl.semaphore_signal(barrier, inc=1, device_id=at(*step), device_id_type=MESH)
    for dy, dt in MEMBERS:
        pl.semaphore_signal(barrier, inc=1, device_id=member(dy, dt), device_id_type=MESH)
    wanted = ((pkv_hbm, pkv_ref), (akv_hbm, akv_ref), (q_hbm, q_ref), (g_hbm, g_ref))
    loads = [pltpu.make_async_copy(*pair, load_sem.at[i]) for i, pair in enumerate(wanted)]
    for load in loads:
        load.start()
    live = len_ref[0]
    tile = one_hot_tile(ap_ref[0])
    hot[OWN] = tile
    pl.semaphore_wait(barrier, OWN + len(MEMBERS))

    def hot_copy(k):
        return pltpu.make_async_remote_copy(
            src_ref=hot.at[OWN],
            dst_ref=hot.at[k],
            send_sem=hs.at[k],
            recv_sem=hr.at[k],
            device_id=at(*CTX_STEPS[k]),
            device_id_type=MESH,
        )

    for k in range(OWN):
        hot_copy(k).start()
    loads[1].wait()
    kt[:, PK:] = scaled_halves(akv_ref[:, :D]).T
    vt[:, PK:] = akv_ref[:, D:].T
    keys[PK:, :] = akv_ref[:, :D]
    for load in loads[2:]:
        load.wait()

    def prepare_heads(i, carry):
        for h in range(4):
            prepare(4 * i + h, q_ref, g_ref, qt, gt, live)
        return carry

    lax.fori_loop(0, heads // 4, prepare_heads, 0)

    def pick_copy(k):
        return pltpu.make_async_remote_copy(
            src_ref=pick.at[k],
            dst_ref=chosen.at[ctx],
            send_sem=ps.at[k],
            recv_sem=pr.at[k],
            device_id=at(*CTX_STEPS[k]),
            device_id_type=MESH,
        )

    def choose(weights):
        total = pkv_ref[0] * weight_row(weights, 0).astype(BF)
        for p in range(1, NP):
            total = total + pkv_ref[p] * weight_row(weights, p).astype(BF)
        return total

    def back(k):
        dz, dx, dc = CTX_STEPS[k]
        return CTX_STEPS.index(((4 - dz) % 4, dx, dc))

    loads[0].wait()
    for k in reversed(range(OWN)):
        hot_copy(back(k)).wait_recv()
        pick[k] = choose(hot[back(k)])
        pick_copy(k).start()
    chosen[ctx] = choose(tile)

    def table_copy(i):
        return pltpu.make_async_remote_copy(
            src_ref=hot,
            dst_ref=hot_all.at[i],
            send_sem=ts.at[i],
            recv_sem=tr.at[i],
            device_id={"samp": samp_at(i)},
            device_id_type=MESH,
        )

    for i in (2, 1, 3):
        table_copy(i).start()

    def own_heads(i, carry):
        for h in range(4):
            own_products(4 * i + h, q_ref, g_ref, kt, vt, s_own, d_own, probs, dscores)
        return carry

    lax.fori_loop(0, heads // 4, own_heads, 0)

    def arrange(first_ctx):
        pair = jnp.concatenate([chosen[first_ctx], chosen[first_ctx + 1]], axis=0)
        start = pl.multiple_of(first_ctx * BL, 2 * BL)
        keys[pl.ds(start, 2 * BL), :] = pair[:, :D]
        kt[:, pl.ds(start, 2 * BL)] = scaled_halves(pair[:, :D]).T
        vt[:, pl.ds(start, 2 * BL)] = pair[:, D:].T

    for k in (14, 12, 4, 6, 8, 10, 0, 2):
        for one in (k, k + 1):
            if one != OWN:
                pick_copy(one).wait_recv()
        dz, dx, _ = CTX_STEPS[k]
        sender = lax.rem(z + 4 - dz, 4) * 4 + lax.rem(xh + dx, 2) * 2
        arrange(sender)

    products(0, q_ref, g_ref, kt, vt, s0, d0)

    def step(h, now, later):
        after = jnp.minimum(h + 1, heads - 1)
        products(after, q_ref, g_ref, kt, vt, *later)
        softmax_terms(h, *now, s_own, d_own, probs, dscores)

    buffers = ((s0, d0), (s1, d1))

    def some_heads(i, carry):
        for h in range(UNROLL):
            step(i * UNROLL + h, buffers[h % 2], buffers[(h + 1) % 2])
        return carry

    lax.fori_loop(0, heads // UNROLL, some_heads, 0)

    def piece_copy(k, i):
        dz, dx, dc = CTX_STEPS[k]
        row = ctx_at(dz, dx, dc) * BL + samp_at(i) * PIECE
        return pltpu.make_async_remote_copy(
            src_ref=grads.at[pl.ds(pl.multiple_of(row, PIECE), PIECE)],
            dst_ref=land.at[k, i],
            send_sem=bs.at[k, i],
            recv_sem=br.at[k, i],
            device_id=at(dz, dx, dc, i),
            device_id_type=MESH,
        )

    def key_value_grads(columns):
        key_grad = jnp.dot(qt[...], dscores[:, columns], preferred_element_type=F32) * SCALE
        value_grad = jnp.dot(gt[...], probs[:, columns], preferred_element_type=F32)
        return key_grad.T.astype(BF), value_grad.T.astype(BF)

    for first in range(0, OWN, 4):
        start = pl.multiple_of(lax.rem(z + CTX_STEPS[first][0], 4) * 256, 256)
        key_grad, value_grad = key_value_grads(pl.ds(start, 256))
        grads[pl.ds(start, 256), :D] = key_grad
        grads[pl.ds(start, 256), D:] = value_grad
        for k in range(first, first + 4):
            for i in SAMP_STEPS:
                if (k, i) != (OWN, 0):
                    piece_copy(k, i).start()
    row = pl.multiple_of(ctx * BL + samp * PIECE, PIECE)
    land[OWN, 0] = grads[pl.ds(row, PIECE), :]

    key_grad, value_grad = key_value_grads(slice(PK, NK))
    mine_kv[:, :D] = key_grad
    mine_kv[:, D:] = value_grad
    mate_copy = pltpu.make_async_remote_copy(
        src_ref=mine_kv,
        dst_ref=mate_kv,
        send_sem=xs,
        recv_sem=xr,
        device_id={"tp": 1 - tp},
        device_id_type=MESH,
    )
    mate_copy.start()

    groups = heads // GROUP

    def query_loop(i, carry):
        rows = pl.ds(pl.multiple_of(i * GROUP * T, GROUP * T), GROUP * T)
        grad = jnp.dot(dscores[rows, :], keys[...], preferred_element_type=F32) * SCALE
        for h in range(GROUP):
            dq[:, head_cols(i * GROUP + h)] = grad[h * T : (h + 1) * T, :]
        return carry

    lax.fori_loop(0, groups // 2, query_loop, 0)
    for i in (2, 1, 3):
        table_copy(i).wait_recv()
    hot_all[0] = hot[...]
    def piece_wait(k, i):
        return pltpu.make_async_remote_copy(
            src_ref=grads.at[pl.ds(0, PIECE)],
            dst_ref=land.at[k, i],
            send_sem=bs.at[k, i],
            recv_sem=br.at[k, i],
            device_id={"tp": 1 - tp},
            device_id_type=MESH,
        )

    def add_step(k, sums):
        for i in SAMP_STEPS:
            block = land[k, i].astype(F32)
            weights = hot_all[i, k]
            sums = tuple(s + block * weight_row(weights, p) for p, s in enumerate(sums))
        return sums

    def arrived(k, sums):
        for i in SAMP_STEPS:
            piece_wait(k, i).wait_recv()
        return add_step(k, sums)

    sums = (jnp.zeros((PIECE, 2 * D), F32),) * NP
    sums = lax.fori_loop(0, OWN, arrived, sums)
    for i in SAMP_STEPS[:-1]:
        piece_wait(OWN, i).wait_recv()
    sums = add_step(OWN, sums)
    here = samp * 2 + tp
    for p in range(NP):
        part[p * PIECE : (p + 1) * PIECE, :] = sums[p].astype(BF)
    parts[here] = part[...]

    def part_copy(i):
        return pltpu.make_async_remote_copy(
            src_ref=part,
            dst_ref=parts.at[here],
            send_sem=ms.at[i],
            recv_sem=mr.at[i],
            device_id=member(*MEMBERS[i]),
            device_id_type=MESH,
        )

    for i in range(len(MEMBERS)):
        part_copy(i).start()
    lax.fori_loop(groups // 2, groups, query_loop, 0)
    mate_copy.wait_recv()
    answer_out[...] = mine_kv[...].astype(F32) + mate_kv[...].astype(F32)
    for k in range(OWN):
        hot_copy(k).wait_send()
        pick_copy(k).wait_send()
    for i in (2, 1, 3):
        table_copy(i).wait_send()

    def sent(k, carry):
        for i in SAMP_STEPS:
            piece_wait(k, i).wait_send()
        return carry

    lax.fori_loop(0, OWN, sent, 0)
    for i in SAMP_STEPS[:-1]:
        piece_wait(OWN, i).wait_send()
    mate_copy.wait_send()
    for i in range(len(MEMBERS)):
        part_copy(i).wait()
    for s in range(4):
        both = parts[2 * s].astype(F32) + parts[2 * s + 1].astype(F32)
        for p in range(NP):
            prompt_out[p, s * PIECE : (s + 1) * PIECE, :] = both[p * PIECE : (p + 1) * PIECE, :]


def backward(answer_len, answer_prompt, q, g, akv, pkv):
    heads = q.shape[1] // D
    rows = heads * T
    vmem = pltpu.VMEM
    dma = pltpu.SemaphoreType.DMA
    hbm = pl.BlockSpec(memory_space=pl.ANY)
    return pl.pallas_call(
        functools.partial(fused_kernel, heads),
        out_shape=(
            vmem((T, heads * D), F32),
            vmem((NP, BL, 2 * D), F32),
            vmem((T, 2 * D), F32),
        ),
        in_specs=[SM, SM, hbm, hbm, hbm, hbm],
        out_specs=(VM, VM, VM),
        scratch_shapes=[
            vmem((T, 2 * D), BF),
            vmem((NP, BL, 2 * D), BF),
            vmem((T, heads * D), BF),
            vmem((T, heads * D), BF),
            vmem((D, rows), BF),
            vmem((D, rows), BF),
            vmem((2 * D, NK), BF),
            vmem((D, NK), BF),
            vmem((NK, D), BF),
            vmem((T, PK), F32),
            vmem((heads, T, T), F32),
            vmem((heads, T, T), F32),
            vmem((rows, NK), BF),
            vmem((rows, NK), BF),
            vmem((NC, 8, 128), F32),
            vmem((4, NC, 8, 128), F32),
            vmem((OWN, BL, 2 * D), BF),
            vmem((NC, BL, 2 * D), BF),
            vmem((PK, 2 * D), BF),
            vmem((NC, 4, PIECE, 2 * D), BF),
            vmem((NP * PIECE, 2 * D), BF),
            vmem((NG, NP * PIECE, 2 * D), BF),
            vmem((T, 2 * D), BF),
            vmem((T, 2 * D), BF),
            dma((4,)),
            dma((NC,)), dma((NC,)), dma((NC,)), dma((NC,)),
            dma((4,)), dma((4,)),
            dma((NC, 4)), dma((NC, 4)),
            dma((NG,)), dma((NG,)),
            dma, dma,
        ],
        compiler_params=pltpu.CompilerParams(
            collective_id=0, has_side_effects=True, vmem_limit_bytes=57 * 2**20
        ),
        name="attention_backward",
    )(answer_len, answer_prompt, q, g, akv, pkv)


def place_kernel(*refs):
    count = len(refs) // 2
    ins, outs, sems = refs[:count], refs[count : 2 * count], refs[-1]
    copies = [pltpu.make_async_copy(ins[i], outs[i], sems.at[i]) for i in range(count)]
    for copy in copies:
        copy.start()
    for copy in copies:
        copy.wait()


def place(*arrays):
    hbm = pl.BlockSpec(memory_space=pl.ANY)
    return pl.pallas_call(
        place_kernel,
        out_shape=tuple(jax.ShapeDtypeStruct(a.shape, a.dtype) for a in arrays),
        in_specs=[VM] * len(arrays),
        out_specs=(hbm,) * len(arrays),
        scratch_shapes=[pltpu.SemaphoreType.DMA((len(arrays),))],
        compiler_params=pltpu.CompilerParams(vmem_limit_bytes=8 * 2**20),
        name="place_outputs",
    )(*arrays)


def body(queries, out_grad, answer_kv, prompt_kv, answer_prompt, answer_len):
    dq, prompt_grad, answer_grad = backward(
        answer_len, answer_prompt, queries[0], out_grad[0], answer_kv[0], prompt_kv
    )
    dq, answer_grad, prompt_grad = place(dq, answer_grad, prompt_grad)
    return dq[None], answer_grad[None], prompt_grad


def solution(mesh):
    placed = (
        P(("ctx", "samp"), None, "tp"),
        P(("ctx", "samp"), None, "tp"),
        P(("ctx", "samp"), None, None),
        P(None, "ctx", None),
        P(("ctx", "samp")),
        P(("ctx", "samp")),
    )
    return jax.shard_map(
        body,
        mesh=mesh,
        in_specs=placed,
        out_specs=(
            P(("ctx", "samp"), None, "tp"),
            P(("ctx", "samp"), None, None),
            P(None, "ctx", None),
        ),
        check_vma=False,
    )
```

profile of v0, /device:TPU:1, one launch (start us, length us, event | category | flops | bytes accessed | tf_op | source)
XLA Modules:
  0.0 56.6 jit_solution(12453389560969945647)
XLA Ops:
  1.9 52.8 %attention_backward.1 = (f32[256,3072]{1,0:T(8,128)S(1)}, f32[4,64,256]{2,1,0:T(8,128)S(1)}, f32[256,256]{1,0:T(8,128)S(1)}) custom-call(s32[1]{0:T(128)S(6)} %copy.10.len_ref, s32[1]{0:T(128)S(6)} %copy.9.ap_ref, bf16[256,3072]{1,0:T(8,128)(2,1)} %bitcast.5, bf16[256,3072]{1,0:T(8,128)(2,1)} %bitcast.6, bf16[256,256]{1,0:T(8,128)(2,1)} %bitcast.7, ...), custom_call_target="tpu_custom_call" | custom-call | tf_op jit(solution)/shard_map/attention_backward/pallas_call | solution.py:385
  54.8 1.9 %place_outputs.1 = (f32[256,3072]{1,0:T(8,128)}, f32[256,256]{1,0:T(8,128)}, f32[4,64,256]{2,1,0:T(8,128)}) custom-call(f32[256,3072]{1,0:T(8,128)S(1)} %get-tuple-element.9.refs_0_, f32[256,256]{1,0:T(8,128)S(1)} %get-tuple-element.10.refs_1_, f32[4,64,256]{2,1,0:T(8,128)S(1)} %get-tuple-element.11.refs_2_), custom_call_target="tpu_custom_call" | custom-call | tf_op jit(solution)/shard_map/place_outputs/pallas_call | solution.py:445
where the time goes:
time: 56.7 us; the launch traced here: 56.6 us
  Pallas kernels  54.7 us (96%)
  between operations  1.93 us (3%)
    pallas_call x1, Pallas kernels, backward(): pl.pallas_call(functools.partial(fused_kernel, heads), out_shape=(vmem((T...  52.8 us
    pallas_call x1, Pallas kernels, place(): pl.pallas_call(place_kernel, out_shape=tuple((jax.ShapeDtypeStruct(a.shap...  1.85 us

commit v1 on v0

--- a/solution.py
+++ b/solution.py
@@ -157,7 +157,7 @@
             device_id_type=MESH,
         )
 
-    for k in range(OWN):
+    for k in reversed(range(OWN)):
         hot_copy(k).start()
     loads[1].wait()
     kt[:, PK:] = scaled_halves(akv_ref[:, :D]).T
@@ -210,8 +210,6 @@
             device_id_type=MESH,
         )
 
-    for i in (2, 1, 3):
-        table_copy(i).start()
 
     def own_heads(i, carry):
         for h in range(4):
@@ -235,6 +233,8 @@
         sender = lax.rem(z + 4 - dz, 4) * 4 + lax.rem(xh + dx, 2) * 2
         arrange(sender)
 
+    for i in (2, 1, 3):
+        table_copy(i).start()
     products(0, q_ref, g_ref, kt, vt, s0, d0)
 
     def step(h, now, later):
@@ -268,7 +268,7 @@
         value_grad = jnp.dot(gt[...], probs[:, columns], preferred_element_type=F32)
         return key_grad.T.astype(BF), value_grad.T.astype(BF)
 
-    for first in range(0, OWN, 4):
+    for first in (4, 0, 8, 12):
         start = pl.multiple_of(lax.rem(z + CTX_STEPS[first][0], 4) * 256, 256)
         key_grad, value_grad = key_value_grads(pl.ds(start, 256))
         grads[pl.ds(start, 256), :D] = key_grad

time: 56.7 us -> 56.6 us (level)
  no operation moved by 1% of the time
where the time goes in v1:
time: 56.6 us; the launch traced here: 56.4 us
  Pallas kernels  54.5 us (96%)
  between operations  1.93 us (3%)
    pallas_call x1, Pallas kernels, backward(): pl.pallas_call(functools.partial(fused_kernel, heads), out_shape=(vmem((T...  52.7 us
    pallas_call x1, Pallas kernels, place(): pl.pallas_call(place_kernel, out_shape=tuple((jax.ShapeDtypeStruct(a.shap...  1.85 us

profile of v1, /device:TPU:1, one launch (start us, length us, event | category | flops | bytes accessed | tf_op | source)
XLA Modules:
  0.0 56.4 jit_solution(13698684453278229714)
XLA Ops:
  1.9 52.7 %attention_backward.1 = (f32[256,3072]{1,0:T(8,128)S(1)}, f32[4,64,256]{2,1,0:T(8,128)S(1)}, f32[256,256]{1,0:T(8,128)S(1)}) custom-call(s32[1]{0:T(128)S(6)} %copy.10.len_ref, s32[1]{0:T(128)S(6)} %copy.9.ap_ref, bf16[256,3072]{1,0:T(8,128)(2,1)} %bitcast.5, bf16[256,3072]{1,0:T(8,128)(2,1)} %bitcast.6, bf16[256,256]{1,0:T(8,128)(2,1)} %bitcast.7, ...), custom_call_target="tpu_custom_call" | custom-call | tf_op jit(solution)/shard_map/attention_backward/pallas_call | solution.py:385
  54.6 1.9 %place_outputs.1 = (f32[256,3072]{1,0:T(8,128)}, f32[256,256]{1,0:T(8,128)}, f32[4,64,256]{2,1,0:T(8,128)}) custom-call(f32[256,3072]{1,0:T(8,128)S(1)} %get-tuple-element.9.refs_0_, f32[256,256]{1,0:T(8,128)S(1)} %get-tuple-element.10.refs_1_, f32[4,64,256]{2,1,0:T(8,128)S(1)} %get-tuple-element.11.refs_2_), custom_call_target="tpu_custom_call" | custom-call | tf_op jit(solution)/shard_map/place_outputs/pallas_call | solution.py:445
